TPU v7x, 256 devices: a whole 4x4x8 slice. The times are simulated.
256 devices in a mesh: row: 16 (over z, core), col: 16 (over y, x).
Axes of the slice: x: 4, y: 4, z: 8, core: 2. Of those that a mesh axis runs over, the one named last changes fastest.
Arguments:
- old_factor: float32 [2, 4096, 2, 4096], P(None, 'row', None, 'col'), may hold values from -32 to 32
- panel_block: float32 [2, 4096, 1024], P(None, 'row'), may hold values from -4 to 4, as said below
Outputs:
- panel_factor: float32 [2, 4096, 1024], P(None, 'row', 'col')
Inputs may be any that keep to these rules, and one draw needn't show every extreme that they name: `panel_block`: the two diagonal blocks of 512 x 512 of entries (rows and columns [s * 512, (s + 1) * 512)) are symmetric up to rounding; for s = 0 and 1 the block schur_s[s * 512:(s + 1) * 512, :] is symmetric up to rounding and has no eigenvalue under 0.05.
All inputs are finite; a program needn't handle non-finite values.
Results may differ from a plain program's by a relative error of at most 0.0003.
Values sent between devices are 32-bit elements; how exact they have to be, the bound alone decides.
A program may use at most 64 MiB of HBM per device.

v0:
```python
import jax
import jax.numpy as jnp
from jax import lax
from jax.sharding import PartitionSpec as P


def from_root(block, axis, source):
    block = jnp.where(lax.axis_index(axis) == source, block, jnp.zeros_like(block))
    return lax.psum(block, axis)


def product(left, right):
    return lax.dot_general(
        left,
        right,
        (((1,), (1,)), ((), ())),
        precision=lax.Precision.HIGHEST,
        preferred_element_type=jnp.float32,
    )


def per_device(old_factor, panel_block):
    row_blocks, tile_rows, col_blocks, tile_cols = old_factor.shape
    local_count = row_blocks * tile_rows
    old_tiles = old_factor.reshape(row_blocks, tile_rows, col_blocks * tile_cols)
    old_local = old_tiles.reshape(local_count, col_blocks * tile_cols)
    panel_width = panel_block.shape[2] // 2
    tile_count = panel_width // tile_rows
    my_row = lax.axis_index("row")
    my_col = lax.axis_index("col")
    row_count = lax.axis_size("row")
    col_count = lax.axis_size("col")
    columns = jnp.arange(panel_width, dtype=jnp.int32)
    in_tile = jnp.arange(tile_rows, dtype=jnp.int32)
    kept_rows = panel_block.shape[1]
    block_index = jnp.arange(row_blocks, dtype=jnp.int32)
    global_row = (
        block_index[:, None] * (tile_rows * row_count) + my_row * tile_rows + in_tile[None, :]
    ).reshape(row_blocks * kept_rows)
    panel_rows = panel_block.reshape(row_blocks * kept_rows, 2 * panel_width)

    def owner_rows(section_index):
        pieces = [
            from_root(old_local[:tile_rows], "row", section_index * tile_count + offset)
            for offset in range(tile_count)
        ]
        return jnp.concatenate(pieces, axis=0)

    def reduce_update(band_rows):
        return lax.psum(product(old_local, band_rows), "col")

    def first_tile(rows):
        return rows[:tile_rows]

    def factor(schur_block, section_index):
        tile_top = first_tile(schur_block)
        pieces = [
            from_root(tile_top, "row", section_index * tile_count + offset)
            for offset in range(tile_count)
        ]
        diagonal = jnp.concatenate(pieces, axis=0)
        cholesky_lower = jnp.linalg.cholesky(diagonal)
        solved = jax.scipy.linalg.solve_triangular(cholesky_lower, schur_block.T, lower=True).T
        keep_mask = columns[None, :] <= (global_row - section_index * panel_width)[:, None]
        return jnp.where(keep_mask, solved, jnp.zeros_like(solved))

    first_factor = factor(panel_rows[:, :panel_width] - reduce_update(owner_rows(0)), 0)
    second_update = reduce_update(owner_rows(1))
    prior_top = first_tile(first_factor)
    prior_pieces = [
        from_root(prior_top, "row", tile_count + offset) for offset in range(tile_count)
    ]
    prior_rows = jnp.concatenate(prior_pieces, axis=0)
    schur_second = panel_rows[:, panel_width:] - second_update - product(first_factor, prior_rows)
    second_factor = factor(schur_second, 1)
    joined = jnp.concatenate([first_factor, second_factor], axis=1)
    width_share = joined.shape[1] // col_count
    own_columns = lax.dynamic_slice_in_dim(joined, my_col * width_share, width_share, 1)
    return own_columns.reshape(row_blocks, tile_rows, width_share)


def solution(mesh):
    return jax.shard_map(
        per_device,
        mesh=mesh,
        in_specs=(P(None, "row", None, "col"), P(None, "row", None)),
        out_specs=P(None, "row", "col"),
        check_vma=False,
    )
```

profile of v0, /device:TPU:64, one launch (start us, length us, event | category | flops | bytes accessed | tf_op | source)
XLA Modules:
  0.0 879.6 jit_solution(588000222398781718)
XLA Ops:
  6.5 1.7 broadcast_select_fusion.1
  11.7 115.3 %all-reduce.20.cloned.1.call-done = (f32[256,512]{1,0:T(8,128)}, f32[256,512]{1,0:T(8,128)}, f32[256,512]{1,0:T(8,128)}, f32[256,512]{1,0:T(8,128)}) async-done(((f32[256,512]{1,0:T(8,128)}, f32[256,512]{1,0:T(8,128)}, f32[256,512]{1,0:T(8,128)}, f32[256,512]{1,0:T(8,128)}), (f32[256,512]{1,0:T(8,128)}, f32[256,512]{1,0:T(8,128)}, f32[256,512]{1,0:T(8,128)}, ...) | async-done | bytes 2097168 | tf_op jit(solution)/shard_map/psum | solution.py:9
  127.0 4.1 convolution_bitcast_fusion
  131.2 2.8 convolution_bitcast_fusion.1
  134.1 1.2 fusion.77
  135.7 101.4 %all-reduce.12.cloned.1.call-done = (f32[512,512]{0,1:T(8,128)}, f32[512,512]{0,1:T(8,128)}) async-done(((f32[512,512]{0,1:T(8,128)}, f32[512,512]{0,1:T(8,128)}), (f32[512,512]{0,1:T(8,128)}, f32[512,512]{0,1:T(8,128)})) %all-reduce.12.cloned.1.call-update) | async-done | bytes 2097168 | tf_op jit(solution)/shard_map/psum | solution.py:50
  237.0 1.4 sub.13
  240.1 108.8 %all-reduce.18.cloned.1.call-done = (f32[256,512]{0,1:T(8,128)}, f32[256,512]{0,1:T(8,128)}) async-done(((f32[256,512]{0,1:T(8,128)}, f32[256,512]{0,1:T(8,128)}), (f32[256,512]{0,1:T(8,128)}, f32[256,512]{0,1:T(8,128)})) %all-reduce.18.cloned.1.call-update) | async-done | bytes 1048592 | tf_op jit(solution)/shard_map/psum | solution.py:9
  352.7 11.7 %cholesky.286 = f32[128,128]{1,0:T(8,128)S(1)} custom-call(f32[128,128]{1,0:T(8,128)S(1)} %cholesky.426), custom_call_target="Cholesky" | custom-call | tf_op jit(solution)/shard_map/jit(cholesky)/cholesky | solution.py:62
  364.6 9.8 %custom-call.27 = f32[1,128,128]{1,2,0:T(8,128)S(1)} custom-call(f32[1,128,128]{2,1,0:T(8,128)S(1)} %get-tuple-element.86), custom_call_target="InvertDiagBlocksLowerTriangular" | custom-call | tf_op jit(solution)/shard_map/jit(cholesky)/cholesky | solution.py:62
  374.4 1.2 constant_dynamic-update-slice_fusion.7
  375.7 1.3 convolution_subtract_fusion.8
  376.9 11.7 %cholesky.305 = f32[128,128]{1,0:T(8,128)S(1)} custom-call(f32[128,128]{1,0:T(8,128)S(1)} %cholesky.430), custom_call_target="Cholesky" | custom-call | tf_op jit(solution)/shard_map/jit(cholesky)/cholesky | solution.py:62
  388.7 10.0 %custom-call.28 = f32[1,128,128]{1,2,0:T(8,128)S(1)} custom-call(f32[1,128,128]{2,1,0:T(8,128)S(1)} %get-tuple-element.83), custom_call_target="InvertDiagBlocksLowerTriangular" | custom-call | tf_op jit(solution)/shard_map/jit(cholesky)/cholesky | solution.py:62
  398.9 1.3 convolution_subtract_fusion.10
  400.2 11.7 %cholesky.326 = f32[128,128]{1,0:T(8,128)S(1)} custom-call(f32[128,128]{1,0:T(8,128)S(1)} %cholesky.435), custom_call_target="Cholesky" | custom-call | tf_op jit(solution)/shard_map/jit(cholesky)/cholesky | solution.py:62
  412.6 9.8 %custom-call.29 = f32[1,128,128]{1,2,0:T(8,128)S(1)} custom-call(f32[1,128,128]{2,1,0:T(8,128)S(1)} %get-tuple-element.80), custom_call_target="InvertDiagBlocksLowerTriangular" | custom-call | tf_op jit(solution)/shard_map/jit(cholesky)/cholesky | solution.py:62
  423.8 11.7 %cholesky.343 = f32[128,128]{1,0:T(8,128)S(1)} custom-call(f32[128,128]{1,0:T(8,128)S(1)} %convolution_subtract_fusion.12), custom_call_target="Cholesky" | custom-call | tf_op jit(solution)/shard_map/jit(cholesky)/cholesky | solution.py:62
  440.0 7.8 while.4
  440.6 1.3 bitcast_dynamic-update-slice_fusion.4
  442.5 1.3 bitcast_dynamic-update-slice_fusion.4
  444.5 1.3 bitcast_dynamic-update-slice_fusion.4
  446.5 1.3 bitcast_dynamic-update-slice_fusion.4
  447.8 39.3 %custom-call.30 = f32[4,128,128]{1,2,0:T(8,128)S(1)} custom-call(f32[4,128,128]{2,1,0:T(8,128)S(1)} %get-tuple-element.21), custom_call_target="InvertDiagBlocksLowerTriangular" | custom-call | tf_op jit(solution)/shard_map/jit(_solve_triangular)/triangular_solve | solution.py:63
  492.0 111.6 %all-reduce.16.cloned.1.call-done = (f32[256,512]{0,1:T(8,128)}, f32[256,512]{0,1:T(8,128)}) async-done(((f32[256,512]{0,1:T(8,128)}, f32[256,512]{0,1:T(8,128)}), (f32[256,512]{0,1:T(8,128)}, f32[256,512]{0,1:T(8,128)})) %all-reduce.16.cloned.1.call-update) | async-done | bytes 1048592 | tf_op jit(solution)/shard_map/psum | solution.py:9
  603.6 3.4 convolution_subtract_fusion
  608.1 112.0 %all-reduce.14.cloned.1.call-done = (f32[256,512]{0,1:T(8,128)}, f32[256,512]{0,1:T(8,128)}) async-done(((f32[256,512]{0,1:T(8,128)}, f32[256,512]{0,1:T(8,128)}), (f32[256,512]{0,1:T(8,128)}, f32[256,512]{0,1:T(8,128)})) %all-reduce.14.cloned.1.call-update) | async-done | bytes 1048592 | tf_op jit(solution)/shard_map/psum | solution.py:9
  722.4 1.3 copy.10
  723.7 1.4 fusion.11
  726.2 11.7 %cholesky.358 = f32[128,128]{1,0:T(8,128)S(1)} custom-call(f32[128,128]{1,0:T(8,128)S(1)} %cholesky.439), custom_call_target="Cholesky" | custom-call | tf_op jit(solution)/shard_map/jit(cholesky)/cholesky | solution.py:62
  738.1 9.8 %custom-call.31 = f32[1,128,128]{1,2,0:T(8,128)S(1)} custom-call(f32[1,128,128]{2,1,0:T(8,128)S(1)} %get-tuple-element.76), custom_call_target="InvertDiagBlocksLowerTriangular" | custom-call | tf_op jit(solution)/shard_map/jit(cholesky)/cholesky | solution.py:62
  747.9 1.2 constant_dynamic-update-slice_fusion.5
  749.1 1.3 convolution_subtract_fusion.7
  750.4 11.9 %cholesky.377 = f32[128,128]{1,0:T(8,128)S(1)} custom-call(f32[128,128]{1,0:T(8,128)S(1)} %cholesky.443), custom_call_target="Cholesky" | custom-call | tf_op jit(solution)/shard_map/jit(cholesky)/cholesky | solution.py:62
  763.6 9.8 %custom-call.32 = f32[1,128,128]{1,2,0:T(8,128)S(1)} custom-call(f32[1,128,128]{2,1,0:T(8,128)S(1)} %get-tuple-element.73), custom_call_target="InvertDiagBlocksLowerTriangular" | custom-call | tf_op jit(solution)/shard_map/jit(cholesky)/cholesky | solution.py:62
  773.7 1.3 convolution_subtract_fusion.9
  775.0 11.7 %cholesky.398 = f32[128,128]{1,0:T(8,128)S(1)} custom-call(f32[128,128]{1,0:T(8,128)S(1)} %cholesky.448), custom_call_target="Cholesky" | custom-call | tf_op jit(solution)/shard_map/jit(cholesky)/cholesky | solution.py:62
  787.4 9.8 %custom-call.33 = f32[1,128,128]{1,2,0:T(8,128)S(1)} custom-call(f32[1,128,128]{2,1,0:T(8,128)S(1)} %get-tuple-element.70), custom_call_target="InvertDiagBlocksLowerTriangular" | custom-call | tf_op jit(solution)/shard_map/jit(cholesky)/cholesky | solution.py:62
  797.5 1.2 convolution_subtract_fusion.11
  798.7 11.9 %cholesky.415 = f32[128,128]{1,0:T(8,128)S(1)} custom-call(f32[128,128]{1,0:T(8,128)S(1)} %convolution_subtract_fusion.11), custom_call_target="Cholesky" | custom-call | tf_op jit(solution)/shard_map/jit(cholesky)/cholesky | solution.py:62
  815.1 11.7 %while.5 = (s32[]{:T(128)}, f32[512,512]{1,0:T(8,128)}, s32[4,2]{0,1:T(2,128)S(1)}, f32[4,128,128]{2,1,0:T(8,128)S(1)}, s32[]{:T(128)}) while((s32[]{:T(128)}, f32[512,512]{1,0:T(8,128)}, s32[4,2]{0,1:T(2,128)S(1)}, f32[4,128,128]{2,1,0:T(8,128)S(1)}, s32[]{:T(128)}) %tuple.79), condition=%wide.while_cond.clone, body=%wide.while_body.clone.sunk | while | flops 2 | bytes 131181 | solution.py:63
  815.8 2.3 bitcast_dynamic-update-slice_fusion.5
  818.7 2.3 bitcast_dynamic-update-slice_fusion.5
  821.7 2.3 bitcast_dynamic-update-slice_fusion.5
  824.6 2.2 bitcast_dynamic-update-slice_fusion.5
  826.8 39.3 %custom-call.34 = f32[4,128,128]{1,2,0:T(8,128)S(1)} custom-call(f32[4,128,128]{2,1,0:T(8,128)S(1)} %get-tuple-element.22), custom_call_target="InvertDiagBlocksLowerTriangular" | custom-call | tf_op jit(solution)/shard_map/jit(_solve_triangular)/triangular_solve | solution.py:63
  868.2 1.3 convolution_subtract_fusion.1
  870.0 1.6 convolution_subtract_fusion.5
  (110 shorter events, 36.5 us)
Async XLA Ops:
  6.5 120.5 %all-reduce.20.cloned.1.call-start = ((), (), s32[]{:S(2)}) async-start(), calls=%async_computation.4 | async-start | bytes 4194304 | tf_op jit(solution)/shard_map/psum | solution.py:9
  9.9 1.7 copy-start.3
  11.6 225.4 %all-reduce.12.cloned.1.call-start = ((), (), s32[]{:S(2)}) async-start(), calls=%async_computation | async-start | bytes 4194304 | tf_op jit(solution)/shard_map/psum | solution.py:50
  127.0 4.1 copy-start.5
  127.0 4.1 copy-start.6
  131.2 2.9 copy-start.4
  134.0 214.9 %all-reduce.18.cloned.1.call-start = ((), (), s32[]{:S(2)}) async-start(), calls=%async_computation.3 | async-start | bytes 2097152 | tf_op jit(solution)/shard_map/psum | solution.py:9
  239.5 364.0 %all-reduce.16.cloned.1.call-start = ((), (), s32[]{:S(2)}) async-start(), calls=%async_computation.2 | async-start | bytes 2097152 | tf_op jit(solution)/shard_map/psum | solution.py:9
  351.7 1.0 copy-start.2
  490.3 1.4 copy-start
  491.5 228.7 %all-reduce.14.cloned.1.call-start = ((), (), s32[]{:S(2)}) async-start(), calls=%async_computation.1 | async-start | bytes 2097152 | tf_op jit(solution)/shard_map/psum | solution.py:9
  725.2 1.0 copy-start.1
Sparse Core Ops, SparseCore 0:
  11.7 115.2 all-reduce.19
  134.1 102.8 all-reduce.11
  239.7 109.2 all-reduce.17
  491.6 111.8 all-reduce.15
  608.2 111.8 all-reduce.13
where the time goes:
time: 889 us; the launch traced here: 880 us
  waiting for transfers between devices  549 us (62%)
  other arithmetic  247 us (28%)
  local copies, waits for them, and re-layouts  33.9 us (4%)
  matrix products  30.2 us (3%)
  between operations  18.9 us (2%)
    psum x4, waiting for transfers between devices, from_root(): return lax.psum(block, axis)  448 us
    another operation x29, other arithmetic, factor(): cholesky_lower = jnp.linalg.cholesky(diagonal)  158 us
    psum x1, waiting for transfers between devices, reduce_update(): return lax.psum(product(old_local, band_rows), 'col')  101 us
    another operation x5, other arithmetic, factor(): jax.scipy.linalg.solve_triangular(cholesky_lower, schur_block.T, lower=True)  79.9 us
    another operation x27, local copies, waits for them, and re-layouts, factor(): jax.scipy.linalg.solve_triangular(cholesky_lower, schur_block.T, lower=True)  19.4 us
  transfers between devices with their start and end apart: 5, of which 5 were waited for; matrix products, arithmetic and copies ran while one was open for 0% of the time, Pallas kernels for 0%

commit v1 on v0

v1 whole, which is shorter than its diff:
```python
import jax
import jax.numpy as jnp
from jax import lax
from jax.experimental import pallas as pl
from jax.experimental.pallas import tpu as pltpu
from jax.sharding import PartitionSpec as P

F32 = jnp.float32
MESH = pl.DeviceIdType.MESH
BLK = 128
NB = 8
SUPER = 2


def lane(x, k):
    return jnp.broadcast_to(x[:, k : k + 1], (8, BLK))


def sub(x, k):
    return jnp.broadcast_to(x[k : k + 1, :], (8, BLK))


def dot_tn(a, b):
    return lax.dot_general(
        a, b, (((0,), (0,)), ((), ())), precision=lax.Precision.HIGHEST, preferred_element_type=F32
    )


def dot_nt(a, b):
    return lax.dot_general(
        a, b, (((1,), (1,)), ((), ())), precision=lax.Precision.HIGHEST, preferred_element_type=F32
    )


def factor_inverse(read, write):
    idx = lax.broadcasted_iota(jnp.int32, (8, BLK), 0)
    col = lax.broadcasted_iota(jnp.int32, (8, BLK), 1)
    groups = BLK // 8
    m = [read(i) for i in range(groups)]
    w = [jnp.where(col == idx + 8 * i, 1.0, 0.0).astype(F32) for i in range(groups)]
    u = [None] * groups
    uw = [None] * groups
    for g in range(groups):
        sb = g // SUPER
        near = list(range(g + 1, min(groups, SUPER * (sb + 2))))
        t, v = m[g], w[g]
        piv = [lane(t, 8 * g + k) for k in range(8)]
        low = {i: [lane(m[i], 8 * g + k) for k in range(8)] for i in near}
        rows, rows_w, mult = [], [], {i: [] for i in near}
        for k in range(8):
            scale = lax.rsqrt(sub(piv[k], k))
            mk = jnp.where(idx > k, piv[k] * scale, 0.0)
            rk, rwk = sub(t, k) * scale, sub(v, k) * scale
            rows.append(rk)
            rows_w.append(rwk)
            if k < 7:
                t, v = t - mk * rk, v - mk * rwk
            for i in near:
                mult[i].append(low[i][k] * scale)
            for n in range(k + 1, 8):
                q = sub(piv[n], k) * scale
                piv[n] = piv[n] - mk * q
                for i in near:
                    low[i][n] = low[i][n] - mult[i][k] * q
        ug, uwg = rows[0], rows_w[0]
        for k in range(1, 8):
            ug, uwg = jnp.where(idx == k, rows[k], ug), jnp.where(idx == k, rows_w[k], uwg)
        u[g], uw[g] = ug, uwg
        write(g, uwg)
        for i in near:
            a, b = m[i], w[i]
            for k in range(8):
                a, b = a - mult[i][k] * rows[k], b - mult[i][k] * rows_w[k]
            m[i], w[i] = a, b
        first = SUPER * (sb + 2)
        if g % SUPER == SUPER - 1 and first < groups:
            us = jnp.concatenate(u[SUPER * sb : g + 1], axis=0)
            ws = jnp.concatenate(uw[SUPER * sb : g + 1], axis=0)
            eu, ew = dot_tn(us, us), dot_tn(us, ws)
            for i in range(first, groups):
                m[i], w[i] = m[i] - eu[8 * i : 8 * i + 8], w[i] - ew[8 * i : 8 * i + 8]


def kernel(
    a_ref, e_hbm, out_ref,
    band, part, rs1, rs2, drs, dt, cm, winv, stage, outv, ebuf,
    e_sem, ring_s, ring_r, back_s, sib_s, sib_r,
    d_s, d_r, z_s, z_r, g1_s, g1_r, g2_s, g2_r, gs_s, gs_r,
    r1_s, r1_r, r2_s, r2_r, o_s, o_r,
):
    r, c = lax.axis_index("row"), lax.axis_index("col")
    z, q = r // 2, r % 2
    sib = r + 1 - 2 * q
    sf, ss = 1 + 3 * q, 4 - 3 * q
    f, s = (c // sf) % 4, (c // ss) % 4
    place = 4 * s + f

    def slot(cc):
        return 4 * ((cc // sf) % 4) + (cc // ss) % 4

    def col_of(ff, sx):
        return ff * sf + sx * ss

    def remote(src, dst, send, recv, row, colm):
        return pltpu.make_async_remote_copy(
            src_ref=src, dst_ref=dst, send_sem=send, recv_sem=recv, device_id=(row, colm), device_id_type=MESH
        )

    def wait_bytes(ref, sem):
        pltpu.make_async_copy(ref, ref, sem).wait()

    e_copy = pltpu.make_async_copy(e_hbm.at[:, pl.ds(pl.multiple_of(16 * c, 16), 16), :], ebuf, e_sem)
    e_copy.start()

    barrier = pltpu.get_barrier_semaphore()

    def greet(d, carry):
        pl.semaphore_signal(barrier, inc=1, device_id=((r + d) % 16, c), device_id_type=MESH)
        pl.semaphore_signal(barrier, inc=1, device_id=(r, (c + d) % 16), device_id_type=MESH)
        return carry

    lax.fori_loop(1, 16, greet, 0)

    @pl.when(r < 4)
    def _():
        band[0, r] = a_ref[0, 0:256, :]
        band[1, r] = a_ref[1, 0:256, :]

    pl.semaphore_wait(barrier, 30)

    def chain(h, i):
        pos = z if h == 0 else (9 - z) % 8
        nxt, prv = ((z + 1) % 8, (z + 7) % 8) if h == 0 else ((z + 7) % 8, (z + 1) % 8)
        is_a = (i // 4 + jnp.where(pos == 0, 1, 0)) % 2
        tile = (q + 2 - 2 * is_a) if h == 0 else (q + 2 * is_a)
        other = (1 - q + 2 - 2 * is_a) if h == 0 else (1 - q + 2 * is_a)
        k = i % 4
        n = 8 * h + 4 * is_a + k
        rows = pl.ds(pl.multiple_of(64 * k, 64), 64)
        mine, theirs = band.at[h, tile, rows], band.at[h, other, rows]
        fwd = remote(mine, mine, ring_s.at[n], ring_r.at[n], 2 * nxt + q, c)
        back = remote(mine, mine, back_s.at[4 * h + k], ring_r.at[n], 2 * prv + q, c)
        to_sib = remote(mine, mine, sib_s.at[n], sib_r.at[n], sib, c)
        from_sib = remote(theirs, theirs, sib_s.at[n], sib_r.at[n], sib, c)
        origin = pos == 1 - is_a
        forwards = jnp.logical_and(pos < 7, pos + is_a > 0)
        returns = jnp.logical_and(pos == 1, is_a == 0)
        return fwd, back, to_sib, from_sib, origin, forwards, returns

    def ring_step(i, carry):
        for h in (0, 1):
            fwd, back, to_sib, _, origin, forwards, returns = chain(h, i)

            @pl.when(jnp.logical_not(origin))
            def _():
                fwd.wait_recv()

            @pl.when(forwards)
            def _():
                fwd.start()

            @pl.when(returns)
            def _():
                back.start()

            to_sib.start()
        return carry

    lax.fori_loop(0, 8, ring_step, 0)

    def ring_end(i, carry):
        for h in (0, 1):
            fwd, back, to_sib, from_sib, origin, forwards, returns = chain(h, i)

            @pl.when(forwards)
            def _():
                fwd.wait_send()

            @pl.when(returns)
            def _():
                back.wait_send()

            to_sib.wait_send()
            from_sib.wait_recv()
        return carry

    lax.fori_loop(0, 8, ring_end, 0)

    def product(i, carry):
        n, tl = i // 2, i % 2
        rows = pl.ds(pl.multiple_of(256 * tl, 256), 256)
        res = dot_nt(a_ref[0, rows, :], band[0, n]) + dot_nt(a_ref[1, rows, :], band[1, n])
        for cc in range(16):
            part[slot(cc), n, pl.ds(pl.multiple_of(16 * tl, 16), 16), :] = res[16 * cc : 16 * cc + 16]
        return carry

    lax.fori_loop(0, 8, product, 0)
    e_copy.wait()

    def d_send(u, d):
        cc = (c + d) % 16
        return remote(part.at[slot(cc), u, pl.ds(0, 16)], drs.at[u, d - 1], d_s.at[u], d_r.at[u], r, cc)

    for u in range(4):

        @pl.when(jnp.logical_and(r < 4, u <= r))
        def _():
            def one(d, carry):
                d_send(u, d).start()
                return carry

            lax.fori_loop(1, 16, one, 0)

    own_rows = pl.ds(pl.multiple_of(16 * place, 16), 16)
    for u in range(4):

        @pl.when(jnp.logical_and(r < 4, u <= r))
        def _():
            wait_bytes(drs.at[u], d_r.at[u])
            total = part[slot(c), u, 0:16, :]
            for k in range(15):
                total = total + drs[u, k]
            dt[r, u, own_rows, :] = ebuf[0, :, 256 * u : 256 * u + 256] - total
            piece = dt.at[r, u, own_rows]

            def one(d, carry):
                remote(piece, piece, z_s.at[u], z_r.at[u // 4 + r // 2, u], 2 * ((z + d) % 8) + q, c).start()
                return carry

            lax.fori_loop(1, 8, one, 0)

    def tiles(fn):
        for tt in (0, 1):
            for u in range(4):
                t = 2 * tt + q

                @pl.when(u <= t)
                def _():
                    fn(tt, t, u)

    def gather1(tt, t, u):
        piece = dt.at[t, u, own_rows]

        @pl.when(r != t)
        def _():
            remote(piece, piece, z_s.at[u], z_r.at[tt, u], sib, c).wait_recv()

        for d in (1, 2, 3):
            remote(piece, piece, g1_s.at[tt, u], g1_r.at[tt, u], r, col_of((f + d) % 4, s)).start()

    line = pl.ds(pl.multiple_of(64 * s, 64), 64)

    def gather2(tt, t, u):
        wait_bytes(dt.at[t, u, pl.ds(0, 48)], g1_r.at[tt, u])
        piece = dt.at[t, u, line]
        for d in (1, 2, 3):
            remote(piece, piece, g2_s.at[tt, u], g2_r.at[tt, u], r, col_of(f, (s + d) % 4)).start()

    def gather3(tt, t, u):
        wait_bytes(dt.at[t, u, pl.ds(0, 192)], g2_r.at[tt, u])
        remote(dt.at[t, u], dt.at[t, u], gs_s.at[tt, u], gs_r.at[tt, u], sib, c).start()

    tiles(gather1)
    tiles(gather2)
    tiles(gather3)
    for t in range(4):
        for u in range(t + 1):

            @pl.when(q != t % 2)
            def _():
                wait_bytes(dt.at[t, u], gs_r.at[t // 2, u])

    for d in (1, 2, 3):
        ff = (f + d) % 4
        remote(part.at[pl.ds(4 * ff, 4)], rs1.at[d - 1], r1_s, r1_r, r, col_of(ff, s)).start()

    def sum_first():
        wait_bytes(rs1, r1_r)
        for u in range(4):

            @pl.when(jnp.logical_and(r < 4, u <= r))
            def _():
                wait_bytes(drs.at[u], d_s.at[u])

        def one(i, carry):
            k, n = i // 4, i % 4
            part[4 * f + k, n] = part[4 * f + k, n] + (rs1[0, k, n] + rs1[1, k, n] + rs1[2, k, n])
            return carry

        lax.fori_loop(0, 16, one, 0)
        for d in (1, 2, 3):
            sx = (s + d) % 4
            remote(part.at[4 * f + sx], rs2.at[d - 1], r2_s, r2_r, r, col_of(f, sx)).start()

    def sum_second():
        wait_bytes(rs2, r2_r)
        for n in range(4):
            total = part[4 * f + s, n] + (rs2[0, n] + rs2[1, n] + rs2[2, n])
            for tl in (0, 1):
                cm[1024 + 16 * tl : 1040 + 16 * tl, 256 * n : 256 * n + 256] = (
                    ebuf[tl, :, 256 * n : 256 * n + 256] - total[16 * tl : 16 * tl + 16]
                )

    for t in range(4):
        for u in range(t + 1):
            for k in range(16):
                at = k if t % 2 == 0 else (k % 4) * 4 + k // 4
                cm[256 * t + 16 * k : 256 * t + 16 * k + 16, 256 * u : 256 * u + 256] = dt[t, u, 16 * at : 16 * at + 16, :]

    def solve_rows(j):
        x = dot_nt(cm[1024:1056, BLK * j : BLK * j + BLK], winv[j])
        cm[1024:1056, BLK * j : BLK * j + BLK] = x
        if j < NB - 1:
            below = BLK * (j + 1)
            cm[1024:1056, below:1024] = cm[1024:1056, below:1024] - dot_nt(x, cm[below:1024, BLK * j : BLK * j + BLK])

    late = 4

    def block(j, carry):
        cols = pl.ds(pl.multiple_of(BLK * j, BLK), BLK)

        def read(i):
            return cm[pl.ds(pl.multiple_of(BLK * j + 8 * i, 8), 8), cols]

        def write(g, x):
            winv[j, 8 * g : 8 * g + 8, :] = x

        factor_inverse(read, write)
        for n in range(NB):

            @pl.when(j == n)
            def _():
                if n == 2:
                    sum_first()
                if n == late:
                    sum_second()
                    for k in range(late):
                        solve_rows(k)
                top, end = BLK * (n + 1), (1056 if n >= late else 1024)
                x = dot_nt(cm[top:end, BLK * n : BLK * n + BLK], winv[n])
                cm[top:end, BLK * n : BLK * n + BLK] = x
                for kb in range(top, 1024, 256):
                    width = min(256, 1024 - kb)
                    cm[kb:end, kb : kb + width] = cm[kb:end, kb : kb + width] - dot_nt(
                        x[kb - top :], x[kb - top : kb - top + width]
                    )

        return carry

    lax.fori_loop(0, NB, block, 0)

    step = lax.broadcasted_iota(jnp.int32, (16, 64), 0)
    lanes = lax.broadcasted_iota(jnp.int32, (16, 64), 1)
    for tl in (0, 1):
        g0 = (16 * tl + r) * 256 + 16 * c
        for cc in range(16):
            x = cm[1024 + 16 * tl : 1040 + 16 * tl, 64 * cc : 64 * cc + 64]
            stage[cc, tl] = jnp.where(lanes + 64 * cc <= step + g0, x, 0.0)
    my_rows = pl.ds(pl.multiple_of(16 * c, 16), 16)

    def out_send(d):
        cc = (c + d) % 16
        return remote(stage.at[cc], outv.at[:, my_rows], o_s.at[d - 1], o_r.at[d - 1], r, cc)

    def out_start(d, carry):
        out_send(d).start()
        return carry

    lax.fori_loop(1, 16, out_start, 0)
    outv[:, my_rows] = stage[c]

    def sent_u(u):
        wait_bytes(dt.at[0, 0, pl.ds(0, 112)], z_s.at[u])

    for u in range(4):

        @pl.when(jnp.logical_and(r < 4, u <= r))
        def _():
            sent_u(u)

    def sent_t(tt, t, u):
        wait_bytes(dt.at[t, u, pl.ds(0, 48)], g1_s.at[tt, u])
        wait_bytes(dt.at[t, u, pl.ds(0, 192)], g2_s.at[tt, u])
        wait_bytes(dt.at[t, u], gs_s.at[tt, u])

    tiles(sent_t)
    wait_bytes(rs1, r1_s)
    wait_bytes(rs2, r2_s)

    def out_end(d, carry):
        copy = out_send(d)
        copy.wait_send()
        copy.wait_recv()
        return carry

    lax.fori_loop(1, 16, out_end, 0)
    out_ref[...] = outv[...]


def per_device(old_factor, panel_block):
    a = jnp.stack([old_factor[:, :, 0, :].reshape(512, 256), old_factor[:, :, 1, :].reshape(512, 256)])
    dma = pltpu.SemaphoreType.DMA
    scratch = [
        pltpu.VMEM((2, 4, 256, 256), F32),
        pltpu.VMEM((16, 4, 32, 256), F32),
        pltpu.VMEM((3, 4, 4, 32, 256), F32),
        pltpu.VMEM((3, 4, 32, 256), F32),
        pltpu.VMEM((4, 15, 16, 256), F32),
        pltpu.VMEM((4, 4, 256, 256), F32),
        pltpu.VMEM((1056, 1024), F32),
        pltpu.VMEM((NB, BLK, BLK), F32),
        pltpu.VMEM((16, 2, 16, 64), F32),
        pltpu.VMEM((2, 256, 64), F32),
        pltpu.VMEM((2, 16, 1024), F32),
        dma, dma((16,)), dma((16,)), dma((8,)), dma((16,)), dma((16,)),
        dma((4,)), dma((4,)), dma((4,)), dma((2, 4)), dma((2, 4)), dma((2, 4)), dma((2, 4)), dma((2, 4)), dma((2, 4)), dma((2, 4)),
        dma, dma, dma, dma, dma((15,)), dma((15,)),
    ]
    return pl.pallas_call(
        kernel,
        out_shape=jax.ShapeDtypeStruct((2, 256, 64), F32),
        in_specs=[pl.BlockSpec(memory_space=pltpu.VMEM), pl.BlockSpec(memory_space=pl.ANY)],
        out_specs=pl.BlockSpec(memory_space=pltpu.VMEM),
        scratch_shapes=scratch,
        compiler_params=pltpu.CompilerParams(
            collective_id=0, has_side_effects=True, vmem_limit_bytes=48 * 1024 * 1024
        ),
    )(a, panel_block)


def solution(mesh):
    return jax.shard_map(
        per_device,
        mesh=mesh,
        in_specs=(P(None, "row", None, "col"), P(None, "row", None)),
        out_specs=P(None, "row", "col"),
        check_vma=False,
    )
```

time: 889 us -> 362 us (0.41); the launches traced: 880 us -> 362 us
  waiting for transfers between devices: 549 us -> 0 us
  Pallas kernels: 0 us -> 357 us
  other arithmetic: 247 us -> 0.07 us
  matrix products: 30.2 us -> 0 us
  local copies, waits for them, and re-layouts: 33.9 us -> 4.81 us
  between operations: 18.9 us -> 0.04 us
    psum x5 -> x0, waiting for transfers between devices: 549 us -> none  [the longest x4 448 us: from_root(): return lax.psum(block, axis)]
    pallas_call x0 -> x1, Pallas kernels: none -> 357 us  [per_device(): pl.pallas_call(kernel, out_shape=jax.ShapeDtypeStruct((2, 256, 64), F32),...]
    another operation x34 -> x1, other arithmetic: 238 us -> 0.07 us  [per_device(): jnp.stack([old_factor[:, :, 0, :].reshape(512, 256), old_factor[:, :, 1,...]
    another operation x26 -> x0, matrix products: 19.8 us -> none  [the longest x12 10.9 us: factor(): cholesky_lower = jnp.linalg.cholesky(diagonal)]
    another operation x35 -> x0, local copies, waits for them, and re-layouts: 19.7 us -> none  [the longest x27 19.4 us: factor(): jax.scipy.linalg.solve_triangular(cholesky_lower, schur_block.T, lower=True)]
    dot_general x3 -> x0, matrix products: 10.4 us -> none  [product(): lax.dot_general(left, right, (((1,), (1,)), ((), ())), precision=lax.Prec...]
  transfers between devices with their start and end apart: 5 -> 0, of which waited for: 5 -> 0; matrix products, arithmetic and copies ran while one was open for 0% -> 0% of each run, Pallas kernels for 0% -> 0%
where the time goes in v1:
time: 362 us
  Pallas kernels  357 us (99%)
  local copies, waits for them, and re-layouts  4.81 us (1%)
    pallas_call x1, Pallas kernels, per_device(): pl.pallas_call(kernel, out_shape=jax.ShapeDtypeStruct((2, 256, 64), F32),...  357 us

profile of v1, /device:TPU:64, one launch (start us, length us, event | category | flops | bytes accessed | tf_op | source)
XLA Modules:
  0.0 362.3 jit_solution(9477322201097568492)
XLA Ops:
  0.0 2.5 fusion
  2.6 0.0 copy-start
  2.7 0.1 pad_maximum_fusion.a_ref
  2.7 1.4 copy-done
  4.1 357.3 %shard_map.28 = f32[2,256,64]{2,1,0:T(8,128)S(1)} custom-call(f32[2,512,256]{2,1,0:T(8,128)S(1)} %pad_maximum_fusion.a_ref, f32[2,256,1024]{2,1,0:T(8,128)S(1)} %copy-done), custom_call_target="tpu_custom_call" | custom-call | tf_op jit(solution)/shard_map/pallas_call | solution.py:419
  361.5 0.8 copy.6
  (2 shorter events, 0.1 us)
Async XLA Ops:
  2.6 1.6 copy-start

commit v2 on v1

--- a/solution.py
+++ b/solution.py
@@ -147,26 +147,33 @@
         returns = jnp.logical_and(pos == 1, is_a == 0)
         return fwd, back, to_sib, from_sib, origin, forwards, returns
 
-    def ring_step(i, carry):
+    def ring_step(tick, carry):
         for h in (0, 1):
-            fwd, back, to_sib, _, origin, forwards, returns = chain(h, i)
-
-            @pl.when(jnp.logical_not(origin))
-            def _():
-                fwd.wait_recv()
-
-            @pl.when(forwards)
-            def _():
-                fwd.start()
-
-            @pl.when(returns)
-            def _():
-                back.start()
-
-            to_sib.start()
-        return carry
-
-    lax.fori_loop(0, 8, ring_step, 0)
+            pos = z if h == 0 else (9 - z) % 8
+            late_by = jnp.maximum(pos - 1, 0)
+            i = jnp.clip(tick - late_by, 0, 7)
+
+            @pl.when(jnp.logical_and(tick >= late_by, tick < late_by + 8))
+            def _():
+                fwd, back, to_sib, _, origin, forwards, returns = chain(h, i)
+
+                @pl.when(jnp.logical_not(origin))
+                def _():
+                    fwd.wait_recv()
+
+                @pl.when(forwards)
+                def _():
+                    fwd.start()
+
+                @pl.when(returns)
+                def _():
+                    back.start()
+
+                to_sib.start()
+
+        return carry
+
+    lax.fori_loop(0, 14, ring_step, 0)
 
     def ring_end(i, carry):
         for h in (0, 1):

time: 362 us -> 131 us (0.36)
  Pallas kernels: 357 us -> 126 us
    pallas_call x1, Pallas kernels: 357 us -> 126 us  [per_device(): pl.pallas_call(kernel, out_shape=jax.ShapeDtypeStruct((2, 256, 64), F32),...]
where the time goes in v2:
time: 131 us
  Pallas kernels  126 us (96%)
  local copies, waits for them, and re-layouts  4.81 us (4%)
    pallas_call x1, Pallas kernels, per_device(): pl.pallas_call(kernel, out_shape=jax.ShapeDtypeStruct((2, 256, 64), F32),...  126 us

profile of v2, /device:TPU:64, one launch (start us, length us, event | category | flops | bytes accessed | tf_op | source)
XLA Modules:
  0.0 130.6 jit_solution(11689544438112409199)
XLA Ops:
  0.0 2.5 %fusion = (f32[2,256,1,256]{3,2,1,0:T(1,128)S(1)}, f32[2,256,1,256]{3,2,1,0:T(1,128)S(1)}) fusion(f32[2,256,2,256]{3,2,1,0:T(2,128)} %param.2), kind=kLoop, calls=%fused_computation.1 | loop fusion | bytes 2097152 | tf_op jit(solution)/shard_map/slice | solution.py:408
  2.6 0.0 copy-start
  2.7 0.1 pad_maximum_fusion.a_ref
  2.7 1.4 %copy-done = f32[2,256,1024]{2,1,0:T(8,128)S(1)} copy-done((f32[2,256,1024]{2,1,0:T(8,128)S(1)}, f32[2,256,1024]{2,1,0:T(8,128)}, u32[]{:S(2)}) %copy-start) | copy-done | bytes 2097176
  4.1 125.6 %shard_map.28 = f32[2,256,64]{2,1,0:T(8,128)S(1)} custom-call(f32[2,512,256]{2,1,0:T(8,128)S(1)} %pad_maximum_fusion.a_ref, f32[2,256,1024]{2,1,0:T(8,128)S(1)} %copy-done), custom_call_target="tpu_custom_call" | custom-call | tf_op jit(solution)/shard_map/pallas_call | solution.py:426
  129.8 0.8 copy.6
  (2 shorter events, 0.1 us)
Async XLA Ops:
  2.6 1.6 %copy-start = (f32[2,256,1024]{2,1,0:T(8,128)S(1)}, f32[2,256,1024]{2,1,0:T(8,128)}, u32[]{:S(2)}) copy-start(f32[2,256,1024]{2,1,0:T(8,128)} %e_hbm.1) | copy-start | bytes 6291460

commit v3 on v2

v3 whole, which is shorter than its diff:
```python
import jax
import jax.numpy as jnp
from jax import lax
from jax.experimental import pallas as pl
from jax.experimental.pallas import tpu as pltpu
from jax.sharding import PartitionSpec as P

F32 = jnp.float32
MESH = pl.DeviceIdType.MESH
BLK = 128
NB = 8
SUPER = 2
NCH = 4
LAG = 3


def lane(x, k):
    return jnp.broadcast_to(x[:, k : k + 1], (8, BLK))


def sub(x, k):
    return jnp.broadcast_to(x[k : k + 1, :], (8, BLK))


def dot_tn(a, b):
    return lax.dot_general(
        a, b, (((0,), (0,)), ((), ())), precision=lax.Precision.HIGHEST, preferred_element_type=F32
    )


def dot_nt(a, b):
    return lax.dot_general(
        a, b, (((1,), (1,)), ((), ())), precision=lax.Precision.HIGHEST, preferred_element_type=F32
    )


def factor_inverse(read, write, poll=None):
    idx = lax.broadcasted_iota(jnp.int32, (8, BLK), 0)
    col = lax.broadcasted_iota(jnp.int32, (8, BLK), 1)
    groups = BLK // 8
    m = [read(i) for i in range(groups)]
    w = [jnp.where(col == idx + 8 * i, 1.0, 0.0).astype(F32) for i in range(groups)]
    u = [None] * groups
    uw = [None] * groups
    for g in range(groups):
        sb = g // SUPER
        near = list(range(g + 1, min(groups, SUPER * (sb + 2))))
        t, v = m[g], w[g]
        piv = [lane(t, 8 * g + k) for k in range(8)]
        low = {i: [lane(m[i], 8 * g + k) for k in range(8)] for i in near}
        rows, rows_w, mult = [], [], {i: [] for i in near}
        for k in range(8):
            scale = lax.rsqrt(sub(piv[k], k))
            mk = jnp.where(idx > k, piv[k] * scale, 0.0)
            rk, rwk = sub(t, k) * scale, sub(v, k) * scale
            rows.append(rk)
            rows_w.append(rwk)
            if k < 7:
                t, v = t - mk * rk, v - mk * rwk
            for i in near:
                mult[i].append(low[i][k] * scale)
            for n in range(k + 1, 8):
                q = sub(piv[n], k) * scale
                piv[n] = piv[n] - mk * q
                for i in near:
                    low[i][n] = low[i][n] - mult[i][k] * q
        ug, uwg = rows[0], rows_w[0]
        for k in range(1, 8):
            ug, uwg = jnp.where(idx == k, rows[k], ug), jnp.where(idx == k, rows_w[k], uwg)
        u[g], uw[g] = ug, uwg
        write(g, uwg)
        for i in near:
            a, b = m[i], w[i]
            for k in range(8):
                a, b = a - mult[i][k] * rows[k], b - mult[i][k] * rows_w[k]
            m[i], w[i] = a, b
        if poll is not None and g % 4 == 3:
            poll(g // 4)
        first = SUPER * (sb + 2)
        if g % SUPER == SUPER - 1 and first < groups:
            us = jnp.concatenate(u[SUPER * sb : g + 1], axis=0)
            ws = jnp.concatenate(uw[SUPER * sb : g + 1], axis=0)
            eu, ew = dot_tn(us, us), dot_tn(us, ws)
            for i in range(first, groups):
                m[i], w[i] = m[i] - eu[8 * i : 8 * i + 8], w[i] - ew[8 * i : 8 * i + 8]


def kernel(
    a_ref, e_hbm, out_ref,
    band, part, rs1, rs2, dpart, drs, cm, winv, stage, outv, ebuf,
    e_sem, ring_s, ring_r, back_s, sib_s, sib_r,
    d_s, d_r, z_s, z_r, g_s, g_r, gs_s, gs_r,
    r1_s, r1_r, r2_s, r2_r, o_s, o_r,
):
    r, c = lax.axis_index("row"), lax.axis_index("col")
    z, q = r // 2, r % 2
    sib = r + 1 - 2 * q
    sf, ss = 1 + 3 * q, 4 - 3 * q
    f, s = (c // sf) % 4, (c // ss) % 4

    def slot(cc):
        return 4 * ((cc // sf) % 4) + (cc // ss) % 4

    def col_of(ff, sx):
        return ff * sf + sx * ss

    def remote(src, dst, send, recv, row, colm):
        return pltpu.make_async_remote_copy(
            src_ref=src, dst_ref=dst, send_sem=send, recv_sem=recv, device_id=(row, colm), device_id_type=MESH
        )

    def wait_bytes(ref, sem):
        pltpu.make_async_copy(ref, ref, sem).wait()

    e_copy = pltpu.make_async_copy(e_hbm.at[:, pl.ds(pl.multiple_of(16 * c, 16), 16), :], ebuf, e_sem)
    e_copy.start()

    barrier = pltpu.get_barrier_semaphore()

    def greet(d, carry):
        pl.semaphore_signal(barrier, inc=1, device_id=(r, (c + d) % 16), device_id_type=MESH)
        return carry

    pl.semaphore_signal(barrier, inc=1, device_id=(sib, c), device_id_type=MESH)
    for d in range(1, 8):
        pl.semaphore_signal(barrier, inc=1, device_id=(2 * ((z + d) % 8) + q, c), device_id_type=MESH)
    lax.fori_loop(1, 16, greet, 0)

    @pl.when(r < 4)
    def _():
        low, high = a_ref[0, 0:256, :], a_ref[1, 0:256, :]
        band[0, r] = low
        band[1, r] = high
        dpart[r] = dot_nt(low, low) + dot_nt(high, high)

    e_copy.wait()
    pl.semaphore_wait(barrier, 23)

    def chain(h, i):
        pos = z if h == 0 else (9 - z) % 8
        nxt, prv = ((z + 1) % 8, (z + 7) % 8) if h == 0 else ((z + 7) % 8, (z + 1) % 8)
        is_a = (i // NCH + jnp.where(pos == 0, 1, 0)) % 2
        tile = (q + 2 - 2 * is_a) if h == 0 else (q + 2 * is_a)
        k = i % NCH
        n = 2 * NCH * h + NCH * is_a + k
        mine = band.at[h, tile, pl.ds(pl.multiple_of(256 // NCH * k, 256 // NCH), 256 // NCH)]
        fwd = remote(mine, mine, ring_s.at[n], ring_r.at[n], 2 * nxt + q, c)
        back = remote(mine, mine, back_s.at[NCH * h + k], ring_r.at[n], 2 * prv + q, c)
        to_sib = remote(mine, mine, sib_s.at[n], sib_r.at[n], sib, c)
        origin = pos == 1 - is_a
        forwards = jnp.logical_and(pos < 7, pos + is_a > 0)
        returns = jnp.logical_and(pos == 1, is_a == 0)
        return fwd, back, to_sib, origin, forwards, returns

    def ring_step(tick, carry):
        for h in (0, 1):
            pos = z if h == 0 else (9 - z) % 8
            late_by = LAG * jnp.maximum(pos - 1, 0)
            i = jnp.clip(tick - late_by, 0, 2 * NCH - 1)

            @pl.when(jnp.logical_and(tick >= late_by, tick < late_by + 2 * NCH))
            def _():
                fwd, back, to_sib, origin, forwards, returns = chain(h, i)

                @pl.when(jnp.logical_not(origin))
                def _():
                    fwd.wait_recv()

                @pl.when(forwards)
                def _():
                    fwd.start()

                @pl.when(returns)
                def _():
                    back.start()

                to_sib.start()

        return carry

    def ring(first, last):
        lax.fori_loop(first, last, ring_step, 0)

    def from_sibling(second):
        def one(k, carry):
            for h in (0, 1):
                is_a = 1 - second if h == 0 else second
                n = 2 * NCH * h + NCH * is_a + k
                theirs = band.at[h, 1 - q + 2 * second, pl.ds(pl.multiple_of(256 // NCH * k, 256 // NCH), 256 // NCH)]
                remote(theirs, theirs, sib_s.at[n], sib_r.at[n], sib, c).wait_recv()
            return carry

        lax.fori_loop(0, NCH, one, 0)

    def ring_end():
        def one(i, carry):
            for h in (0, 1):
                fwd, back, to_sib, origin, forwards, returns = chain(h, i)

                @pl.when(forwards)
                def _():
                    fwd.wait_send()

                @pl.when(returns)
                def _():
                    back.wait_send()

                to_sib.wait_send()
            return carry

        lax.fori_loop(0, 2 * NCH, one, 0)

        @pl.when(z > 1)
        def _():
            from_sibling(0)

        @pl.when(z != 1)
        def _():
            from_sibling(1)

    def d_send(u, d):
        cc = (c + d) % 16
        rows = pl.ds(pl.multiple_of(16 * cc, 16), 16)
        return remote(dpart.at[u, rows], drs.at[u, d - 1], d_s.at[u], d_r.at[u], r, cc)

    def d_start(u):
        def one(d, carry):
            d_send(u, d).start()
            return carry

        lax.fori_loop(1, 16, one, 0)

    def d_rest(owner):
        @pl.when(r == owner)
        def _():
            for u in range(owner):
                dpart[u] = dot_nt(a_ref[0, 0:256, :], band[0, u]) + dot_nt(a_ref[1, 0:256, :], band[1, u])
                d_start(u)

    def piece_of(t, u):
        rows = pl.ds(pl.multiple_of(256 * t + 16 * c, 16), 16)
        return cm.at[rows, pl.ds(256 * u, 256)]

    def tile_of(t, u):
        return cm.at[pl.ds(pl.multiple_of(256 * t, 256), 256), pl.ds(256 * u, 256)]

    def rows_of(n):
        return cm.at[pl.ds(0, n), pl.ds(0, 256)]

    def sum_tiles(tt):
        for u in range(2 * tt + 2):

            @pl.when(jnp.logical_and(z == tt, u <= r))
            def _():
                wait_bytes(drs.at[u], d_r.at[u])
                total = dpart[u, pl.ds(pl.multiple_of(16 * c, 16), 16), :]
                for k in range(15):
                    total = total + drs[u, k]
                piece = piece_of(r, u)
                piece[...] = ebuf[0, :, 256 * u : 256 * u + 256] - total

                def one(d, carry):
                    remote(piece, piece, z_s.at[u], z_r.at[tt, u], 2 * ((z + d) % 8) + q, c).start()
                    return carry

                lax.fori_loop(1, 8, one, 0)

    def tiles(tt, fn):
        for u in range(2 * tt + 2):
            t = 2 * tt + q

            @pl.when(u <= t)
            def _():
                fn(tt, t, u)

    def gather(tt, t, u):
        piece = piece_of(t, u)

        @pl.when(r != t)
        def _():
            remote(piece, piece, z_s.at[u], z_r.at[tt, u], sib, c).wait_recv()

        def one(d, carry):
            remote(piece, piece, g_s.at[tt, u], g_r.at[tt, u], r, (c + d) % 16).start()
            return carry

        lax.fori_loop(1, 16, one, 0)

    def share(tt, t, u):
        wait_bytes(rows_of(240), g_r.at[tt, u])
        tile = tile_of(t, u)
        remote(tile, tile, gs_s.at[tt, u], gs_r.at[tt, u], sib, c).start()

    def shared(tt):
        for u in range(2 * tt + 2):
            t = 2 * tt + 1 - q

            @pl.when(u <= t)
            def _():
                wait_bytes(rows_of(256), gs_r.at[tt, u])

    def sent(tt):
        def one(tt, t, u):
            wait_bytes(rows_of(240), g_s.at[tt, u])
            wait_bytes(rows_of(256), gs_s.at[tt, u])

        tiles(tt, one)
        for u in range(2 * tt + 2):

            @pl.when(jnp.logical_and(z == tt, u <= r))
            def _():
                wait_bytes(drs.at[u], d_s.at[u])
                wait_bytes(rows_of(112), z_s.at[u])

    def product(i, carry):
        n, tl = i // 2, i % 2
        rows = pl.ds(pl.multiple_of(256 * tl, 256), 256)
        res = dot_nt(a_ref[0, rows, :], band[0, n]) + dot_nt(a_ref[1, rows, :], band[1, n])
        for cc in range(16):
            part[slot(cc), n, pl.ds(pl.multiple_of(16 * tl, 16), 16), :] = res[16 * cc : 16 * cc + 16]
        return carry

    def products():
        lax.fori_loop(0, 8, product, 0)
        for d in (1, 2, 3):
            ff = (f + d) % 4
            remote(part.at[pl.ds(4 * ff, 4)], rs1.at[d - 1], r1_s, r1_r, r, col_of(ff, s)).start()

    def sum_first():
        wait_bytes(rs1, r1_r)

        def one(i, carry):
            k, n = i // 4, i % 4
            part[4 * f + k, n] = part[4 * f + k, n] + (rs1[0, k, n] + rs1[1, k, n] + rs1[2, k, n])
            return carry

        lax.fori_loop(0, 16, one, 0)
        for d in (1, 2, 3):
            sx = (s + d) % 4
            remote(part.at[4 * f + sx], rs2.at[d - 1], r2_s, r2_r, r, col_of(f, sx)).start()

    def sum_second():
        wait_bytes(rs2, r2_r)
        for n in range(4):
            total = part[4 * f + s, n] + (rs2[0, n] + rs2[1, n] + rs2[2, n])
            for tl in (0, 1):
                cm[1024 + 16 * tl : 1040 + 16 * tl, 256 * n : 256 * n + 256] = (
                    ebuf[tl, :, 256 * n : 256 * n + 256] - total[16 * tl : 16 * tl + 16]
                )

    def solve_rows(j):
        x = dot_nt(cm[1024:1056, BLK * j : BLK * j + BLK], winv[j])
        cm[1024:1056, BLK * j : BLK * j + BLK] = x
        if j < NB - 1:
            below = BLK * (j + 1)
            cm[1024:1056, below:1024] = cm[1024:1056, below:1024] - dot_nt(x, cm[below:1024, BLK * j : BLK * j + BLK])

    def blocks(first, last, bottom, rows_from, ticks, after):
        def block(j, carry):
            cols = pl.ds(pl.multiple_of(BLK * j, BLK), BLK)

            def read(i):
                return cm[pl.ds(pl.multiple_of(BLK * j + 8 * i, 8), 8), cols]

            def write(g, x):
                winv[j, 8 * g : 8 * g + 8, :] = x

            def poll(n):
                ring(ticks + 4 * j + n, ticks + 4 * j + n + 1)

            factor_inverse(read, write, poll if ticks else None)
            for n in range(first, last):

                @pl.when(j == n)
                def _():
                    if n == rows_from:
                        for k in range(n):
                            solve_rows(k)
                    top, end = BLK * (n + 1), (1056 if n >= rows_from else bottom)
                    if top < end:
                        x = dot_nt(cm[top:end, BLK * n : BLK * n + BLK], winv[n])
                        cm[top:end, BLK * n : BLK * n + BLK] = x
                        for kb in range(top, bottom, 256):
                            width = min(256, bottom - kb)
                            cm[kb:end, kb : kb + width] = cm[kb:end, kb : kb + width] - dot_nt(
                                x[kb - top :], x[kb - top : kb - top + width]
                            )
                    after(n)

            return carry

        lax.fori_loop(first, last, block, 0)

    @pl.when(r < 4)
    def _():
        d_start(r)

    ring(0, 4)

    @pl.when(z == 0)
    def _():
        from_sibling(0)

    d_rest(1)
    ring(4, 7)
    sum_tiles(0)
    ring(7, 10)
    tiles(0, gather)

    @pl.when(z == 1)
    def _():
        from_sibling(0)
        from_sibling(1)

    d_rest(2)
    d_rest(3)
    ring(10, 12)
    tiles(0, share)
    ring(12, 14)
    sum_tiles(1)
    shared(0)
    sent(0)

    def after_first(n):
        if n == 0:
            tiles(1, gather)
        if n == 2:
            ring_end()
            products()
            tiles(1, share)
        if n == 3:
            shared(1)
            sent(1)

    blocks(0, 4, 512, NB, 14, after_first)

    for k in range(4):
        x = dot_nt(cm[512:1024, BLK * k : BLK * k + BLK], winv[k])
        cm[512:1024, BLK * k : BLK * k + BLK] = x
        if k < 3:
            below = BLK * (k + 1)
            cm[512:1024, below:512] = cm[512:1024, below:512] - dot_nt(x, cm[below:512, BLK * k : BLK * k + BLK])
    for kb in (512, 768):
        cm[kb:1024, kb : kb + 256] = cm[kb:1024, kb : kb + 256] - dot_nt(cm[kb:1024, 0:512], cm[kb : kb + 256, 0:512])

    def after_second(n):
        if n == 4:
            sum_first()
        if n == 5:
            sum_second()

    blocks(4, 8, 1024, 6, 0, after_second)

    step = lax.broadcasted_iota(jnp.int32, (16, 64), 0)
    lanes = lax.broadcasted_iota(jnp.int32, (16, 64), 1)
    for tl in (0, 1):
        g0 = (16 * tl + r) * 256 + 16 * c
        for cc in range(16):
            x = cm[1024 + 16 * tl : 1040 + 16 * tl, 64 * cc : 64 * cc + 64]
            stage[cc, tl] = jnp.where(lanes + 64 * cc <= step + g0, x, 0.0)
    my_rows = pl.ds(pl.multiple_of(16 * c, 16), 16)

    def out_send(d):
        cc = (c + d) % 16
        return remote(stage.at[cc], outv.at[:, my_rows], o_s.at[d - 1], o_r.at[d - 1], r, cc)

    def out_start(d, carry):
        out_send(d).start()
        return carry

    lax.fori_loop(1, 16, out_start, 0)
    outv[:, my_rows] = stage[c]

    wait_bytes(rs1, r1_s)
    wait_bytes(rs2, r2_s)

    def out_end(d, carry):
        copy = out_send(d)
        copy.wait_send()
        copy.wait_recv()
        return carry

    lax.fori_loop(1, 16, out_end, 0)
    out_ref[...] = outv[...]


def per_device(old_factor, panel_block):
    a = jnp.transpose(old_factor, (2, 0, 1, 3)).reshape(2, 512, 256)
    dma = pltpu.SemaphoreType.DMA
    scratch = [
        pltpu.VMEM((2, 4, 256, 256), F32),
        pltpu.VMEM((16, 4, 32, 256), F32),
        pltpu.VMEM((3, 4, 4, 32, 256), F32),
        pltpu.VMEM((3, 4, 32, 256), F32),
        pltpu.VMEM((4, 256, 256), F32),
        pltpu.VMEM((4, 15, 16, 256), F32),
        pltpu.VMEM((1056, 1024), F32),
        pltpu.VMEM((NB, BLK, BLK), F32),
        pltpu.VMEM((16, 2, 16, 64), F32),
        pltpu.VMEM((2, 256, 64), F32),
        pltpu.VMEM((2, 16, 1024), F32),
        dma, dma((4 * NCH,)), dma((4 * NCH,)), dma((2 * NCH,)), dma((4 * NCH,)), dma((4 * NCH,)),
        dma((4,)), dma((4,)), dma((4,)), dma((2, 4)), dma((2, 4)), dma((2, 4)), dma((2, 4)), dma((2, 4)),
        dma, dma, dma, dma, dma((15,)), dma((15,)),
    ]
    return pl.pallas_call(
        kernel,
        out_shape=jax.ShapeDtypeStruct((2, 256, 64), F32),
        in_specs=[pl.BlockSpec(memory_space=pltpu.VMEM), pl.BlockSpec(memory_space=pl.ANY)],
        out_specs=pl.BlockSpec(memory_space=pltpu.VMEM),
        scratch_shapes=scratch,
        compiler_params=pltpu.CompilerParams(
            collective_id=0, has_side_effects=True, vmem_limit_bytes=60 * 1024 * 1024
        ),
    )(a, panel_block)


def solution(mesh):
    return jax.shard_map(
        per_device,
        mesh=mesh,
        in_specs=(P(None, "row", None, "col"), P(None, "row", None)),
        out_specs=P(None, "row", "col"),
        check_vma=False,
    )
```

time: 131 us -> 104 us (0.79)
  Pallas kernels: 126 us -> 98.7 us
    pallas_call x1, Pallas kernels: 126 us -> 98.7 us  [per_device(): pl.pallas_call(kernel, out_shape=jax.ShapeDtypeStruct((2, 256, 64), F32),...]
    slice x1 -> x0, local copies, waits for them, and re-layouts: 2.55 us -> none  [per_device(): old_factor[:, :, 0, :].reshape(512, 256)]
    transpose x0 -> x1, local copies, waits for them, and re-layouts: none -> 2.31 us  [per_device(): a = jnp.transpose(old_factor, (2, 0, 1, 3)).reshape(2, 512, 256)]
    unnamed x4 -> x0, local copies, waits for them, and re-layouts: 1.49 us -> none
where the time goes in v3:
time: 104 us; the launch traced here: 103 us
  Pallas kernels  98.7 us (95%)
  local copies, waits for them, and re-layouts  4.04 us (4%)
    pallas_call x1, Pallas kernels, per_device(): pl.pallas_call(kernel, out_shape=jax.ShapeDtypeStruct((2, 256, 64), F32),...  98.7 us
    transpose x1, local copies, waits for them, and re-layouts, per_device(): a = jnp.transpose(old_factor, (2, 0, 1, 3)).reshape(2, 512, 256)  2.31 us

profile of v3, /device:TPU:64, one launch (start us, length us, event | category | flops | bytes accessed | tf_op | source)
XLA Modules:
  0.0 102.8 jit_solution(3993155808622414455)
XLA Ops:
  0.0 2.3 %copy.3 = f32[2,2,256,256]{3,2,1,0:T(8,128)} copy(f32[2,2,256,256]{3,0,2,1:T(2,128)} %bitcast.3) | data formatting | bytes 2097152 | tf_op jit(solution)/shard_map/transpose | solution.py:488
  2.3 98.7 %shard_map.28 = f32[2,256,64]{2,1,0:T(8,128)} custom-call(f32[2,512,256]{2,1,0:T(8,128)} %bitcast.2, f32[2,256,1024]{2,1,0:T(8,128)} %e_hbm.1), custom_call_target="tpu_custom_call" | custom-call | tf_op jit(solution)/shard_map/pallas_call | solution.py:506
  101.1 1.7 %copy.4 = f32[2,256,64]{1,2,0:T(8,128)} copy(f32[2,256,64]{2,1,0:T(8,128)} %shard_map.28) | data formatting | bytes 262144 | tf_op jit(solution)/shard_map/pallas_call | solution.py:506

commit v4 on v3

--- a/solution.py
+++ b/solution.py
@@ -31,6 +31,12 @@
 def dot_nt(a, b):
     return lax.dot_general(
         a, b, (((1,), (1,)), ((), ())), precision=lax.Precision.HIGHEST, preferred_element_type=F32
+    )
+
+
+def dot_nn(a, b):
+    return lax.dot_general(
+        a, b, (((1,), (0,)), ((), ())), precision=lax.Precision.HIGHEST, preferred_element_type=F32
     )
 
 
@@ -87,7 +93,7 @@
 
 def kernel(
     a_ref, e_hbm, out_ref,
-    band, part, rs1, rs2, dpart, drs, cm, winv, stage, outv, ebuf,
+    band, part, rs1, rs2, dpart, drs, cm, winv, wide_inv, stage, outv, ebuf,
     e_sem, ring_s, ring_r, back_s, sib_s, sib_r,
     d_s, d_r, z_s, z_r, g_s, g_r, gs_s, gs_r,
     r1_s, r1_r, r2_s, r2_r, o_s, o_r,
@@ -131,7 +137,12 @@
         low, high = a_ref[0, 0:256, :], a_ref[1, 0:256, :]
         band[0, r] = low
         band[1, r] = high
-        dpart[r] = dot_nt(low, low) + dot_nt(high, high)
+        own = dot_nt(low, low) + dot_nt(high, high)
+        for t in range(4):
+
+            @pl.when(r == t)
+            def _():
+                dpart[:, 256 * t : 256 * t + 256] = own
 
     e_copy.wait()
     pl.semaphore_wait(barrier, 23)
@@ -218,99 +229,73 @@
         def _():
             from_sibling(1)
 
-    def d_send(u, d):
-        cc = (c + d) % 16
-        rows = pl.ds(pl.multiple_of(16 * cc, 16), 16)
-        return remote(dpart.at[u, rows], drs.at[u, d - 1], d_s.at[u], d_r.at[u], r, cc)
-
-    def d_start(u):
+    def wide(t):
+        return pl.ds(0, 256 * (t + 1))
+
+    def at(where, fn, t):
+        @pl.when(where)
+        def _():
+            fn(t)
+
+    def d_start(t):
         def one(d, carry):
-            d_send(u, d).start()
+            cc = (c + d) % 16
+            rows = pl.ds(pl.multiple_of(16 * cc, 16), 16)
+            remote(dpart.at[rows, wide(t)], drs.at[d - 1, :, wide(t)], d_s, d_r, r, cc).start()
             return carry
 
         lax.fori_loop(1, 16, one, 0)
 
-    def d_rest(owner):
-        @pl.when(r == owner)
-        def _():
-            for u in range(owner):
-                dpart[u] = dot_nt(a_ref[0, 0:256, :], band[0, u]) + dot_nt(a_ref[1, 0:256, :], band[1, u])
-                d_start(u)
-
-    def piece_of(t, u):
-        rows = pl.ds(pl.multiple_of(256 * t + 16 * c, 16), 16)
-        return cm.at[rows, pl.ds(256 * u, 256)]
-
-    def tile_of(t, u):
-        return cm.at[pl.ds(pl.multiple_of(256 * t, 256), 256), pl.ds(256 * u, 256)]
-
-    def rows_of(n):
-        return cm.at[pl.ds(0, n), pl.ds(0, 256)]
-
-    def sum_tiles(tt):
-        for u in range(2 * tt + 2):
-
-            @pl.when(jnp.logical_and(z == tt, u <= r))
-            def _():
-                wait_bytes(drs.at[u], d_r.at[u])
-                total = dpart[u, pl.ds(pl.multiple_of(16 * c, 16), 16), :]
-                for k in range(15):
-                    total = total + drs[u, k]
-                piece = piece_of(r, u)
-                piece[...] = ebuf[0, :, 256 * u : 256 * u + 256] - total
-
-                def one(d, carry):
-                    remote(piece, piece, z_s.at[u], z_r.at[tt, u], 2 * ((z + d) % 8) + q, c).start()
-                    return carry
-
-                lax.fori_loop(1, 8, one, 0)
-
-    def tiles(tt, fn):
-        for u in range(2 * tt + 2):
-            t = 2 * tt + q
-
-            @pl.when(u <= t)
-            def _():
-                fn(tt, t, u)
-
-    def gather(tt, t, u):
-        piece = piece_of(t, u)
+    def d_rest(t):
+        for u in range(t):
+            dpart[:, 256 * u : 256 * u + 256] = dot_nt(a_ref[0, 0:256, :], band[0, u]) + dot_nt(
+                a_ref[1, 0:256, :], band[1, u]
+            )
+        d_start(t)
+
+    def piece_of(t):
+        return cm.at[pl.ds(pl.multiple_of(256 * t + 16 * c, 16), 16), wide(t)]
+
+    def sum_tiles(t):
+        width = 256 * (t + 1)
+        wait_bytes(drs.at[:, :, wide(t)], d_r)
+        total = dpart[pl.ds(pl.multiple_of(16 * c, 16), 16), 0:width]
+        for k in range(15):
+            total = total + drs[k, :, 0:width]
+        piece = piece_of(t)
+        piece[...] = ebuf[0, :, 0:width] - total
+        for d in range(1, 8):
+            remote(piece, piece, z_s, z_r.at[t // 2], 2 * ((z + d) % 8) + q, c).start()
+
+    def gather(t):
+        piece = piece_of(t)
 
         @pl.when(r != t)
         def _():
-            remote(piece, piece, z_s.at[u], z_r.at[tt, u], sib, c).wait_recv()
+            remote(piece, piece, z_s, z_r.at[t // 2], sib, c).wait_recv()
 
         def one(d, carry):
-            remote(piece, piece, g_s.at[tt, u], g_r.at[tt, u], r, (c + d) % 16).start()
+            remote(piece, piece, g_s.at[t // 2], g_r.at[t // 2], r, (c + d) % 16).start()
             return carry
 
         lax.fori_loop(1, 16, one, 0)
 
-    def share(tt, t, u):
-        wait_bytes(rows_of(240), g_r.at[tt, u])
-        tile = tile_of(t, u)
-        remote(tile, tile, gs_s.at[tt, u], gs_r.at[tt, u], sib, c).start()
-
-    def shared(tt):
-        for u in range(2 * tt + 2):
-            t = 2 * tt + 1 - q
-
-            @pl.when(u <= t)
-            def _():
-                wait_bytes(rows_of(256), gs_r.at[tt, u])
-
-    def sent(tt):
-        def one(tt, t, u):
-            wait_bytes(rows_of(240), g_s.at[tt, u])
-            wait_bytes(rows_of(256), gs_s.at[tt, u])
-
-        tiles(tt, one)
-        for u in range(2 * tt + 2):
-
-            @pl.when(jnp.logical_and(z == tt, u <= r))
-            def _():
-                wait_bytes(drs.at[u], d_s.at[u])
-                wait_bytes(rows_of(112), z_s.at[u])
+    def share(t):
+        wait_bytes(cm.at[pl.ds(0, 240), wide(t)], g_r.at[t // 2])
+        rows = cm.at[pl.ds(256 * t, 256), wide(t)]
+        remote(rows, rows, gs_s.at[t // 2], gs_r.at[t // 2], sib, c).start()
+
+    def shared(t):
+        wait_bytes(cm.at[pl.ds(0, 256), wide(t)], gs_r.at[t // 2])
+
+    def sent(t):
+        wait_bytes(cm.at[pl.ds(0, 240), wide(t)], g_s.at[t // 2])
+        wait_bytes(cm.at[pl.ds(0, 256), wide(t)], gs_s.at[t // 2])
+
+        @pl.when(r == t)
+        def _():
+            wait_bytes(drs.at[:, :, wide(t)], d_s)
+            wait_bytes(cm.at[pl.ds(0, 112), wide(t)], z_s)
 
     def product(i, carry):
         n, tl = i // 2, i % 2
@@ -348,52 +333,71 @@
                     ebuf[tl, :, 256 * n : 256 * n + 256] - total[16 * tl : 16 * tl + 16]
                 )
 
-    def solve_rows(j):
-        x = dot_nt(cm[1024:1056, BLK * j : BLK * j + BLK], winv[j])
-        cm[1024:1056, BLK * j : BLK * j + BLK] = x
-        if j < NB - 1:
-            below = BLK * (j + 1)
-            cm[1024:1056, below:1024] = cm[1024:1056, below:1024] - dot_nt(x, cm[below:1024, BLK * j : BLK * j + BLK])
-
-    def blocks(first, last, bottom, rows_from, ticks, after):
-        def block(j, carry):
-            cols = pl.ds(pl.multiple_of(BLK * j, BLK), BLK)
-
-            def read(i):
-                return cm[pl.ds(pl.multiple_of(BLK * j + 8 * i, 8), 8), cols]
-
-            def write(g, x):
-                winv[j, 8 * g : 8 * g + 8, :] = x
-
-            def poll(n):
-                ring(ticks + 4 * j + n, ticks + 4 * j + n + 1)
-
-            factor_inverse(read, write, poll if ticks else None)
-            for n in range(first, last):
-
-                @pl.when(j == n)
-                def _():
-                    if n == rows_from:
-                        for k in range(n):
-                            solve_rows(k)
-                    top, end = BLK * (n + 1), (1056 if n >= rows_from else bottom)
-                    if top < end:
-                        x = dot_nt(cm[top:end, BLK * n : BLK * n + BLK], winv[n])
-                        cm[top:end, BLK * n : BLK * n + BLK] = x
-                        for kb in range(top, bottom, 256):
-                            width = min(256, bottom - kb)
-                            cm[kb:end, kb : kb + width] = cm[kb:end, kb : kb + width] - dot_nt(
-                                x[kb - top :], x[kb - top : kb - top + width]
-                            )
-                    after(n)
+    def rows_solved(top, bottom, p, end):
+        left, below = 256 * p, 256 * (p + 1)
+        x = dot_nt(cm[top:bottom, left:below], wide_inv[p])
+        cm[top:bottom, left:below] = x
+        if below < end:
+            cm[top:bottom, below:end] = cm[top:bottom, below:end] - dot_nt(x, cm[below:end, left:below])
+
+    def pair_inverse(p):
+        w0, w1 = winv[2 * p], winv[2 * p + 1]
+        mid = dot_nn(cm[256 * p + 128 : 256 * p + 256, 256 * p : 256 * p + 128], w0)
+        wide_inv[p, 0:128, 0:128] = w0
+        wide_inv[p, 0:128, 128:256] = jnp.zeros((128, 128), F32)
+        wide_inv[p, 128:256, 0:128] = -dot_nn(w1, mid)
+        wide_inv[p, 128:256, 128:256] = w1
+
+    def before_pair(t):
+        top = 256 * t
+        for p in range(t):
+            rows_solved(top, top + 256, p, top)
+        x = cm[top : top + 256, 0:top]
+        cm[top : top + 256, top : top + 256] = cm[top : top + 256, top : top + 256] - dot_nt(x, x)
+
+    def after_block(n):
+        if n % 2 == 0:
+            top, left = BLK * (n + 1), BLK * n
+            x = dot_nt(cm[top : top + BLK, left:top], winv[n])
+            cm[top : top + BLK, left:top] = x
+            cm[top : top + BLK, top : top + BLK] = cm[top : top + BLK, top : top + BLK] - dot_nt(x, x)
+        elif n < NB - 1:
+            pair_inverse(n // 2)
+
+    def own_rows_solved():
+        for p in range(3):
+            rows_solved(1024, 1056, p, 1024)
+        x = dot_nt(cm[1024:1056, 768:896], winv[6])
+        cm[1024:1056, 768:896] = x
+        cm[1024:1056, 896:1024] = cm[1024:1056, 896:1024] - dot_nt(x, cm[896:1024, 768:896])
+
+    step = lax.broadcasted_iota(jnp.int32, (16, 64), 0)
+    lanes = lax.broadcasted_iota(jnp.int32, (16, 64), 1)
+    my_rows = pl.ds(pl.multiple_of(16 * c, 16), 16)
+
+    def out_send(d):
+        cc = (c + d) % 16
+        return remote(stage.at[cc], outv.at[:, my_rows], o_s.at[d - 1], o_r.at[d - 1], r, cc)
+
+    def out_start(first, last):
+        for tl in (0, 1):
+            g0 = (16 * tl + r) * 256 + 16 * c
+            for cc in range(first, last):
+                x = cm[1024 + 16 * tl : 1040 + 16 * tl, 64 * cc : 64 * cc + 64]
+                stage[cc, tl] = jnp.where(lanes + 64 * cc <= step + g0, x, 0.0)
+
+        def one(cc, carry):
+            @pl.when(cc != c)
+            def _():
+                out_send((cc - c + 16) % 16).start()
 
             return carry
 
-        lax.fori_loop(first, last, block, 0)
-
-    @pl.when(r < 4)
+        lax.fori_loop(first, last, one, 0)
+
+    @pl.when(r == 0)
     def _():
-        d_start(r)
+        d_start(0)
 
     ring(0, 4)
 
@@ -401,74 +405,92 @@
     def _():
         from_sibling(0)
 
-    d_rest(1)
-    ring(4, 7)
-    sum_tiles(0)
-    ring(7, 10)
-    tiles(0, gather)
+        @pl.when(r == 1)
+        def _():
+            d_rest(1)
+
+    at(r == 0, sum_tiles, 0)
+    ring(4, 6)
+    at(q == 0, gather, 0)
+    at(r == 1, sum_tiles, 1)
+    ring(6, 8)
+    at(q == 0, share, 0)
 
     @pl.when(z == 1)
     def _():
         from_sibling(0)
         from_sibling(1)
 
-    d_rest(2)
-    d_rest(3)
-    ring(10, 12)
-    tiles(0, share)
-    ring(12, 14)
-    sum_tiles(1)
-    shared(0)
-    sent(0)
-
-    def after_first(n):
+    at(r == 2, d_rest, 2)
+    at(r == 3, d_rest, 3)
+    at(q == 1, gather, 1)
+    ring(8, 10)
+    at(q == 1, shared, 0)
+    at(q == 0, sent, 0)
+
+    def before(n):
+        if n == 2:
+            at(q == 0, shared, 1)
+            at(q == 1, sent, 1)
+            at(q == 0, gather, 2)
+            at(q == 1, gather, 3)
+        if n == 4:
+            at(q == 1, shared, 2)
+            at(q == 0, sent, 2)
+        if n == 6:
+            at(q == 0, shared, 3)
+            at(q == 1, sent, 3)
+        before_pair(n // 2)
+
+    def after(n):
+        after_block(n)
         if n == 0:
-            tiles(1, gather)
+            at(q == 1, share, 1)
+            at(r == 2, sum_tiles, 2)
+            at(r == 3, sum_tiles, 3)
         if n == 2:
+            at(q == 0, share, 2)
+            at(q == 1, share, 3)
+        if n == 3:
             ring_end()
             products()
-            tiles(1, share)
-        if n == 3:
-            shared(1)
-            sent(1)
-
-    blocks(0, 4, 512, NB, 14, after_first)
-
-    for k in range(4):
-        x = dot_nt(cm[512:1024, BLK * k : BLK * k + BLK], winv[k])
-        cm[512:1024, BLK * k : BLK * k + BLK] = x
-        if k < 3:
-            below = BLK * (k + 1)
-            cm[512:1024, below:512] = cm[512:1024, below:512] - dot_nt(x, cm[below:512, BLK * k : BLK * k + BLK])
-    for kb in (512, 768):
-        cm[kb:1024, kb : kb + 256] = cm[kb:1024, kb : kb + 256] - dot_nt(cm[kb:1024, 0:512], cm[kb : kb + 256, 0:512])
-
-    def after_second(n):
-        if n == 4:
+        if n == 5:
             sum_first()
-        if n == 5:
+        if n == 6:
             sum_second()
-
-    blocks(4, 8, 1024, 6, 0, after_second)
-
-    step = lax.broadcasted_iota(jnp.int32, (16, 64), 0)
-    lanes = lax.broadcasted_iota(jnp.int32, (16, 64), 1)
-    for tl in (0, 1):
-        g0 = (16 * tl + r) * 256 + 16 * c
-        for cc in range(16):
-            x = cm[1024 + 16 * tl : 1040 + 16 * tl, 64 * cc : 64 * cc + 64]
-            stage[cc, tl] = jnp.where(lanes + 64 * cc <= step + g0, x, 0.0)
-    my_rows = pl.ds(pl.multiple_of(16 * c, 16), 16)
-
-    def out_send(d):
-        cc = (c + d) % 16
-        return remote(stage.at[cc], outv.at[:, my_rows], o_s.at[d - 1], o_r.at[d - 1], r, cc)
-
-    def out_start(d, carry):
-        out_send(d).start()
+            own_rows_solved()
+            out_start(0, 14)
+
+    def block(j, carry):
+        for n in (2, 4, 6):
+
+            @pl.when(j == n)
+            def _():
+                before(n)
+
+        cols = pl.ds(pl.multiple_of(BLK * j, BLK), BLK)
+
+        def read(i):
+            return cm[pl.ds(pl.multiple_of(BLK * j + 8 * i, 8), 8), cols]
+
+        def write(g, x):
+            winv[j, 8 * g : 8 * g + 8, :] = x
+
+        def poll(k):
+            ring(10 + 4 * j + k, 11 + 4 * j + k)
+
+        factor_inverse(read, write, poll)
+        for n in range(NB):
+
+            @pl.when(j == n)
+            def _():
+                after(n)
+
         return carry
 
-    lax.fori_loop(1, 16, out_start, 0)
+    lax.fori_loop(0, NB, block, 0)
+    cm[1024:1056, 896:1024] = dot_nt(cm[1024:1056, 896:1024], winv[7])
+    out_start(14, 16)
     outv[:, my_rows] = stage[c]
 
     wait_bytes(rs1, r1_s)
@@ -492,15 +514,16 @@
         pltpu.VMEM((16, 4, 32, 256), F32),
         pltpu.VMEM((3, 4, 4, 32, 256), F32),
         pltpu.VMEM((3, 4, 32, 256), F32),
-        pltpu.VMEM((4, 256, 256), F32),
-        pltpu.VMEM((4, 15, 16, 256), F32),
+        pltpu.VMEM((256, 1024), F32),
+        pltpu.VMEM((15, 16, 1024), F32),
         pltpu.VMEM((1056, 1024), F32),
         pltpu.VMEM((NB, BLK, BLK), F32),
+        pltpu.VMEM((3, 256, 256), F32),
         pltpu.VMEM((16, 2, 16, 64), F32),
         pltpu.VMEM((2, 256, 64), F32),
         pltpu.VMEM((2, 16, 1024), F32),
         dma, dma((4 * NCH,)), dma((4 * NCH,)), dma((2 * NCH,)), dma((4 * NCH,)), dma((4 * NCH,)),
-        dma((4,)), dma((4,)), dma((4,)), dma((2, 4)), dma((2, 4)), dma((2, 4)), dma((2, 4)), dma((2, 4)),
+        dma, dma, dma, dma((2,)), dma((2,)), dma((2,)), dma((2,)), dma((2,)),
         dma, dma, dma, dma, dma((15,)), dma((15,)),
     ]
     return pl.pallas_call(

time: 104 us -> 114 us (1.096)
  the two profiles are of different devices: /device:TPU:64 before, /device:TPU:28 now
where the time goes in v4:
time: 114 us
  Pallas kernels  110 us (96%)
  local copies, waits for them, and re-layouts  4.04 us (4%)
    pallas_call x1, Pallas kernels, per_device(): pl.pallas_call(kernel, out_shape=jax.ShapeDtypeStruct((2, 256, 64), F32),...  110 us
    transpose x1, local copies, waits for them, and re-layouts, per_device(): a = jnp.transpose(old_factor, (2, 0, 1, 3)).reshape(2, 512, 256)  2.31 us

profile of v4, /device:TPU:28, one launch (start us, length us, event | category | flops | bytes accessed | tf_op | source)
XLA Modules:
  0.0 114.2 jit_solution(12071784292101943595)
XLA Ops:
  0.0 2.3 %copy.3 = f32[2,2,256,256]{3,2,1,0:T(8,128)} copy(f32[2,2,256,256]{3,0,2,1:T(2,128)} %bitcast.3) | data formatting | bytes 2097152 | tf_op jit(solution)/shard_map/transpose | solution.py:510
  2.3 110.2 %shard_map.28 = f32[2,256,64]{2,1,0:T(8,128)} custom-call(f32[2,512,256]{2,1,0:T(8,128)} %bitcast.2, f32[2,256,1024]{2,1,0:T(8,128)} %e_hbm.1), custom_call_target="tpu_custom_call" | custom-call | tf_op jit(solution)/shard_map/pallas_call | solution.py:529
  112.5 1.7 %copy.4 = f32[2,256,64]{1,2,0:T(8,128)} copy(f32[2,256,64]{2,1,0:T(8,128)} %shard_map.28) | data formatting | bytes 262144 | tf_op jit(solution)/shard_map/pallas_call | solution.py:529

commit v5 on v3

--- a/solution.py
+++ b/solution.py
@@ -315,9 +315,24 @@
     def product(i, carry):
         n, tl = i // 2, i % 2
         rows = pl.ds(pl.multiple_of(256 * tl, 256), 256)
-        res = dot_nt(a_ref[0, rows, :], band[0, n]) + dot_nt(a_ref[1, rows, :], band[1, n])
-        for cc in range(16):
-            part[slot(cc), n, pl.ds(pl.multiple_of(16 * tl, 16), 16), :] = res[16 * cc : 16 * cc + 16]
+        known = jnp.logical_and(r < 4, tl == 0)
+
+        @pl.when(jnp.logical_and(known, n <= r))
+        def _():
+            for cc in range(16):
+                part[slot(cc), n, 0:16, :] = dpart[n, 16 * cc : 16 * cc + 16, :]
+
+        @pl.when(jnp.logical_and(known, n > r))
+        def _():
+            for cc in range(16):
+                part[cc, n, 0:16, :] = jnp.zeros((16, 256), F32)
+
+        @pl.when(jnp.logical_not(known))
+        def _():
+            res = dot_nt(a_ref[0, rows, :], band[0, n]) + dot_nt(a_ref[1, rows, :], band[1, n])
+            for cc in range(16):
+                part[slot(cc), n, pl.ds(pl.multiple_of(16 * tl, 16), 16), :] = res[16 * cc : 16 * cc + 16]
+
         return carry
 
     def products():
@@ -443,32 +458,40 @@
     for kb in (512, 768):
         cm[kb:1024, kb : kb + 256] = cm[kb:1024, kb : kb + 256] - dot_nt(cm[kb:1024, 0:512], cm[kb : kb + 256, 0:512])
 
+    step = lax.broadcasted_iota(jnp.int32, (16, 64), 0)
+    lanes = lax.broadcasted_iota(jnp.int32, (16, 64), 1)
+    my_rows = pl.ds(pl.multiple_of(16 * c, 16), 16)
+
+    def out_send(d):
+        cc = (c + d) % 16
+        return remote(stage.at[cc], outv.at[:, my_rows], o_s.at[d - 1], o_r.at[d - 1], r, cc)
+
+    def out_start(first, last):
+        for tl in (0, 1):
+            g0 = (16 * tl + r) * 256 + 16 * c
+            for cc in range(first, last):
+                x = cm[1024 + 16 * tl : 1040 + 16 * tl, 64 * cc : 64 * cc + 64]
+                stage[cc, tl] = jnp.where(lanes + 64 * cc <= step + g0, x, 0.0)
+
+        def one(cc, carry):
+            @pl.when(cc != c)
+            def _():
+                out_send((cc - c + 16) % 16).start()
+
+            return carry
+
+        lax.fori_loop(first, last, one, 0)
+
     def after_second(n):
         if n == 4:
             sum_first()
         if n == 5:
             sum_second()
+        if n == 6:
+            out_start(0, 14)
 
     blocks(4, 8, 1024, 6, 0, after_second)
-
-    step = lax.broadcasted_iota(jnp.int32, (16, 64), 0)
-    lanes = lax.broadcasted_iota(jnp.int32, (16, 64), 1)
-    for tl in (0, 1):
-        g0 = (16 * tl + r) * 256 + 16 * c
-        for cc in range(16):
-            x = cm[1024 + 16 * tl : 1040 + 16 * tl, 64 * cc : 64 * cc + 64]
-            stage[cc, tl] = jnp.where(lanes + 64 * cc <= step + g0, x, 0.0)
-    my_rows = pl.ds(pl.multiple_of(16 * c, 16), 16)
-
-    def out_send(d):
-        cc = (c + d) % 16
-        return remote(stage.at[cc], outv.at[:, my_rows], o_s.at[d - 1], o_r.at[d - 1], r, cc)
-
-    def out_start(d, carry):
-        out_send(d).start()
-        return carry
-
-    lax.fori_loop(1, 16, out_start, 0)
+    out_start(14, 16)
     outv[:, my_rows] = stage[c]
 
     wait_bytes(rs1, r1_s)
@@ -481,7 +504,8 @@
         return carry
 
     lax.fori_loop(1, 16, out_end, 0)
-    out_ref[...] = outv[...]
+    for tl in (0, 1):
+        out_ref[tl] = outv[tl].T
 
 
 def per_device(old_factor, panel_block):
@@ -503,16 +527,17 @@
         dma((4,)), dma((4,)), dma((4,)), dma((2, 4)), dma((2, 4)), dma((2, 4)), dma((2, 4)), dma((2, 4)),
         dma, dma, dma, dma, dma((15,)), dma((15,)),
     ]
-    return pl.pallas_call(
+    out = pl.pallas_call(
         kernel,
-        out_shape=jax.ShapeDtypeStruct((2, 256, 64), F32),
+        out_shape=jax.ShapeDtypeStruct((2, 64, 256), F32),
         in_specs=[pl.BlockSpec(memory_space=pltpu.VMEM), pl.BlockSpec(memory_space=pl.ANY)],
         out_specs=pl.BlockSpec(memory_space=pltpu.VMEM),
         scratch_shapes=scratch,
         compiler_params=pltpu.CompilerParams(
-            collective_id=0, has_side_effects=True, vmem_limit_bytes=60 * 1024 * 1024
+            collective_id=0, has_side_effects=True, vmem_limit_bytes=62 * 1024 * 1024
         ),
     )(a, panel_block)
+    return jnp.transpose(out, (0, 2, 1))
 
 
 def solution(mesh):

time: 104 us -> 99.9 us (0.961)
  Pallas kernels: 98.7 us -> 95.4 us
    pallas_call x1, Pallas kernels: 98.7 us -> 95.4 us  [per_device(): pl.pallas_call(kernel, out_shape=jax.ShapeDtypeStruct((2, 64, 256), F32),...]
    pallas_call x1 -> x0, local copies, waits for them, and re-layouts: 1.72 us -> none  [per_device(): pl.pallas_call(kernel, out_shape=jax.ShapeDtypeStruct((2, 256, 64), F32),...]
    unnamed x0 -> x1, local copies, waits for them, and re-layouts: none -> 1.57 us
where the time goes in v5:
time: 99.9 us; the launch traced here: 99.3 us
  Pallas kernels  95.4 us (95%)
  local copies, waits for them, and re-layouts  3.88 us (4%)
    pallas_call x1, Pallas kernels, per_device(): pl.pallas_call(kernel, out_shape=jax.ShapeDtypeStruct((2, 64, 256), F32),...  95.4 us
    transpose x1, local copies, waits for them, and re-layouts, per_device(): a = jnp.transpose(old_factor, (2, 0, 1, 3)).reshape(2, 512, 256)  2.31 us

profile of v5, /device:TPU:64, one launch (start us, length us, event | category | flops | bytes accessed | tf_op | source)
XLA Modules:
  0.0 99.3 jit_solution(5680229142364755969)
XLA Ops:
  0.0 2.3 %copy.3 = f32[2,2,256,256]{3,2,1,0:T(8,128)} copy(f32[2,2,256,256]{3,0,2,1:T(2,128)} %bitcast.4) | data formatting | bytes 2097152 | tf_op jit(solution)/shard_map/transpose | solution.py:512
  2.3 95.4 %shard_map.28 = f32[2,64,256]{2,1,0:T(8,128)} custom-call(f32[2,512,256]{2,1,0:T(8,128)} %bitcast.3, f32[2,256,1024]{2,1,0:T(8,128)} %e_hbm.1), custom_call_target="tpu_custom_call" | custom-call | tf_op jit(solution)/shard_map/pallas_call | solution.py:530
  97.7 1.6 %copy.5 = f32[2,256,64]{1,2,0:T(8,128)} copy(f32[2,256,64]{1,2,0:T(8,128)} %bitcast.5) | data formatting | bytes 262144

commit v6 on v5

--- a/solution.py
+++ b/solution.py
@@ -46,7 +46,8 @@
         sb = g // SUPER
         near = list(range(g + 1, min(groups, SUPER * (sb + 2))))
         t, v = m[g], w[g]
-        piv = [lane(t, 8 * g + k) for k in range(8)]
+        piv = ahead if g else [lane(t, 8 * g + k) for k in range(8)]
+        ahead = [lane(m[g + 1], 8 * g + 8 + k) for k in range(8)] if g < groups - 1 else None
         low = {i: [lane(m[i], 8 * g + k) for k in range(8)] for i in near}
         rows, rows_w, mult = [], [], {i: [] for i in near}
         for k in range(8):
@@ -59,6 +60,9 @@
                 t, v = t - mk * rk, v - mk * rwk
             for i in near:
                 mult[i].append(low[i][k] * scale)
+            if ahead is not None:
+                lk = mult[g + 1][k]
+                ahead = [ahead[n] - lk * sub(lk, n) for n in range(8)]
             for n in range(k + 1, 8):
                 q = sub(piv[n], k) * scale
                 piv[n] = piv[n] - mk * q

time: 99.9 us -> 97 us (0.971)
  Pallas kernels: 95.4 us -> 92.5 us
    pallas_call x1, Pallas kernels: 95.4 us -> 92.5 us  [per_device(): pl.pallas_call(kernel, out_shape=jax.ShapeDtypeStruct((2, 64, 256), F32),...]
where the time goes in v6:
time: 97 us; the launch traced here: 96.4 us
  Pallas kernels  92.5 us (95%)
  local copies, waits for them, and re-layouts  3.88 us (4%)
    pallas_call x1, Pallas kernels, per_device(): pl.pallas_call(kernel, out_shape=jax.ShapeDtypeStruct((2, 64, 256), F32),...  92.5 us
    transpose x1, local copies, waits for them, and re-layouts, per_device(): a = jnp.transpose(old_factor, (2, 0, 1, 3)).reshape(2, 512, 256)  2.31 us

profile of v6, /device:TPU:64, one launch (start us, length us, event | category | flops | bytes accessed | tf_op | source)
XLA Modules:
  0.0 96.4 jit_solution(2008708110622154609)
XLA Ops:
  0.0 2.3 %copy.3 = f32[2,2,256,256]{3,2,1,0:T(8,128)} copy(f32[2,2,256,256]{3,0,2,1:T(2,128)} %bitcast.4) | data formatting | bytes 2097152 | tf_op jit(solution)/shard_map/transpose | solution.py:516
  2.3 92.5 %shard_map.28 = f32[2,64,256]{2,1,0:T(8,128)} custom-call(f32[2,512,256]{2,1,0:T(8,128)} %bitcast.3, f32[2,256,1024]{2,1,0:T(8,128)} %e_hbm.1), custom_call_target="tpu_custom_call" | custom-call | tf_op jit(solution)/shard_map/pallas_call | solution.py:534
  94.8 1.6 %copy.5 = f32[2,256,64]{1,2,0:T(8,128)} copy(f32[2,256,64]{1,2,0:T(8,128)} %bitcast.5) | data formatting | bytes 262144

commit v7 on v6

--- a/solution.py
+++ b/solution.py
@@ -436,12 +436,13 @@
     ring(10, 12)
     tiles(0, share)
     ring(12, 14)
-    sum_tiles(1)
     shared(0)
     sent(0)
 
     def after_first(n):
         if n == 0:
+            sum_tiles(1)
+        if n == 1:
             tiles(1, gather)
         if n == 2:
             ring_end()

time: 97 us -> 95.8 us (0.988)
  no operation moved by 1% of the time
where the time goes in v7:
time: 95.8 us; the launch traced here: 95.6 us
  Pallas kernels  91.7 us (96%)
  local copies, waits for them, and re-layouts  3.88 us (4%)
    pallas_call x1, Pallas kernels, per_device(): pl.pallas_call(kernel, out_shape=jax.ShapeDtypeStruct((2, 64, 256), F32),...  91.7 us
    transpose x1, local copies, waits for them, and re-layouts, per_device(): a = jnp.transpose(old_factor, (2, 0, 1, 3)).reshape(2, 512, 256)  2.31 us

profile of v7, /device:TPU:64, one launch (start us, length us, event | category | flops | bytes accessed | tf_op | source)
XLA Modules:
  0.0 95.6 jit_solution(667806620046040116)
XLA Ops:
  0.0 2.3 %copy.3 = f32[2,2,256,256]{3,2,1,0:T(8,128)} copy(f32[2,2,256,256]{3,0,2,1:T(2,128)} %bitcast.4) | data formatting | bytes 2097152 | tf_op jit(solution)/shard_map/transpose | solution.py:517
  2.3 91.7 %shard_map.28 = f32[2,64,256]{2,1,0:T(8,128)} custom-call(f32[2,512,256]{2,1,0:T(8,128)} %bitcast.3, f32[2,256,1024]{2,1,0:T(8,128)} %e_hbm.1), custom_call_target="tpu_custom_call" | custom-call | tf_op jit(solution)/shard_map/pallas_call | solution.py:535
  94.0 1.6 %copy.5 = f32[2,256,64]{1,2,0:T(8,128)} copy(f32[2,256,64]{1,2,0:T(8,128)} %bitcast.5) | data formatting | bytes 262144
